TPU v7x, 256 devices: a whole 4x4x8 slice. The times are simulated.
256 devices in a mesh: dp: 16 (over z, core), expert: 16 (over x, y).
Axes of the slice: x: 4, y: 4, z: 8, core: 2. Of those that a mesh axis runs over, the one named last changes fastest.
Arguments:
- history: bfloat16 [512, 1024, 2048], P(('dp', 'expert')), may hold values from -6 to 6
- lengths: int32 [512], P(('dp', 'expert')), may hold values from 64 to 1024, as said below
- user_query: bfloat16 [512, 2048], P(('dp', 'expert')), may hold values from -1000 to 1000
- pos_item: bfloat16 [512, 2048], P(('dp', 'expert')), may hold values from -6 to 6
- neg_index: int32 [512, 63], P(('dp', 'expert')), may hold values from 0 to 511
- routes: int32 [32768, 2], P(('dp', 'expert')), may hold values from 0 to 15, all different within a row; in each aligned block of 128 rows (0 to 127, 128 to 255, ...) at most 32 rows name the same one
- w_router: bfloat16 [2048, 16], replicated, may hold values from -0.125 to 0.125
- w_gate: bfloat16 [16, 2048, 768], P('expert', 'dp'), may hold values from -0.125 to 0.125
- w_up: bfloat16 [16, 2048, 768], P('expert', 'dp'), may hold values from -0.125 to 0.125
- w_down: bfloat16 [16, 768, 2048], P('expert', None, 'dp'), may hold values from -0.21875 to 0.21875
- out_gain: float32 [2048], replicated, may hold values from 0.25 to 1.75
Outputs:
- losses: float32 [512], P(('dp', 'expert'))
- grad_gate: float32 [16, 2048, 768], P('expert', 'dp')
- grad_up: float32 [16, 2048, 768], P('expert', 'dp')
- grad_down: float32 [16, 768, 2048], P('expert', None, 'dp')
- grad_router: float32 [2048, 16], replicated
Inputs may be any that keep to these rules, and one draw needn't show every extreme that they name: `lengths`: every device's block of 2 users holds one user with all 1024 events. `neg_index`: indices of users anywhere in the batch. `routes`: each row names two different experts; among the rows of one device no expert is named more than 32 times, a bound that some block reaches.
All inputs are finite; a program needn't handle non-finite values.
Results may differ from a plain program's by a relative error of at most 0.017.
Values may be sent and summed in bfloat16 or wider, within the bound.
A program may use at most 128 MiB of HBM per device.

v0:
```python
import math
import jax
import jax.numpy as jnp
from jax import lax
from jax.sharding import Mesh
from jax.sharding import PartitionSpec as P

D = 2048
HEADS = 16
HEAD = 128
FF = 768
CANDS = 64
EXPERT = ("expert_0", "expert_1")
DP = ("dp_0", "dp_1")
DP_EXPERT = ("dp_0", "dp_1", "expert_0", "expert_1")
norm_eps = 1e-06
loss_scale = 1024.0


def sent_together(arrays, axis, dim, along):
    widths = [a.shape[along] for a in arrays]
    both = jnp.concatenate(arrays, axis=along)
    result = lax.all_gather(both, axis, axis=dim, tiled=True)
    return tuple(jnp.split(result, [sum(widths[:k]) for k in range(1, len(widths))], axis=along))


def whole_of(x, axes, dim):
    result = x
    for number in range(len(axes) - 1, -1, -1):
        result = lax.all_gather(result, axes[number], axis=dim, tiled=True)
    return result


def over_axes_2(x, axes):
    for axis in axes:
        x = lax.psum(x, axis)
    return x


def silu_pair(pre_act):
    sigma_val = jax.nn.sigmoid(pre_act)
    return (pre_act * sigma_val, sigma_val * (1.0 + pre_act * (1.0 - sigma_val)))


def rms_round(values):
    scale_inv = lax.rsqrt(jnp.mean(values * values, axis=-1, keepdims=True) + norm_eps)
    return (values * scale_inv).astype(jnp.bfloat16)


def local(
    history,
    lengths,
    user_query,
    pos_item,
    neg_index,
    routes,
    w_router,
    w_gate,
    w_up,
    w_down,
    out_gain,
):
    user_count = history.shape[0]
    hist_len = history.shape[1]
    model_width = history.shape[2]
    experts = w_router.shape[1]
    expert_devs = lax.axis_size(EXPERT)
    capacity = 4 * user_count * CANDS // experts
    slot_count = expert_devs * capacity
    row_total = user_count * CANDS
    query_heads = user_query.reshape(user_count, HEADS, HEAD)
    key_heads = history.reshape(user_count, hist_len, HEADS, HEAD)
    scores = jnp.einsum(
        "uhd,uthd->uht", query_heads, key_heads, preferred_element_type=jnp.float32
    ) / math.sqrt(HEAD)
    live_mask = jnp.arange(hist_len, dtype=jnp.int32)[None, None, :] < lengths[:, None, None]
    scores = jnp.where(live_mask, scores, -1e30)
    top_val = jnp.max(scores, axis=-1, keepdims=True)
    weights = jnp.where(live_mask, jnp.exp(scores - top_val), 0.0)
    attn_probs = (weights / jnp.sum(weights, axis=-1, keepdims=True)).astype(jnp.bfloat16)
    context = jnp.einsum(
        "uht,uthd->uhd", attn_probs, key_heads, preferred_element_type=jnp.float32
    ).reshape(user_count, model_width)
    all_items = lax.all_gather(pos_item, DP_EXPERT, axis=0, tiled=True)
    candidates = jnp.concatenate([pos_item[:, None, :], all_items[neg_index]], axis=1)
    x_sum = candidates.astype(jnp.float32) + context[:, None, :]
    normed = rms_round(x_sum).reshape(row_total, model_width)
    logits = jnp.dot(normed, w_router, preferred_element_type=jnp.float32)
    affinity = jax.nn.sigmoid(jnp.take_along_axis(logits, routes, axis=1))
    aff_total = jnp.sum(affinity, axis=1, keepdims=True)
    mix = affinity / aff_total
    flat_routes = routes.reshape(-1)
    one_hot = (flat_routes[:, None] == jnp.arange(experts, dtype=jnp.int32)[None, :]).astype(
        jnp.int32
    )
    slot_rank = jnp.sum(jnp.cumsum(one_hot, axis=0) * one_hot, axis=1) - 1
    slot_dest = flat_routes * capacity + slot_rank
    user_base = (lax.axis_index(DP) * expert_devs + lax.axis_index(EXPERT)) * user_count
    own_users = user_base + jnp.arange(user_count, dtype=jnp.int32)
    item_ids = jnp.concatenate([own_users[:, None], neg_index], axis=1).reshape(-1)
    user_ids = (own_users[:, None] + jnp.zeros((user_count, CANDS), jnp.int32)).reshape(-1)
    item_send = (
        jnp.zeros((experts * capacity,), jnp.int32).at[slot_dest].set(jnp.repeat(item_ids, 2))
    )
    user_send = (
        jnp.full((experts * capacity,), -1, jnp.int32).at[slot_dest].set(jnp.repeat(user_ids, 2))
    )
    item_got, user_got = (
        lax.all_to_all(
            item_send.reshape(experts, capacity), EXPERT, split_axis=0, concat_axis=0, tiled=True
        ),
        lax.all_to_all(
            user_send.reshape(experts, capacity), EXPERT, split_axis=0, concat_axis=0, tiled=True
        ),
    )
    group_ctx = lax.all_gather(context, EXPERT, axis=0, tiled=True)
    user_flat = user_got.reshape(-1)
    live_slot = (user_flat >= 0)[:, None]
    local_user = jnp.maximum(user_flat - lax.axis_index(DP) * expert_devs * user_count, 0)
    rebuilt = all_items[item_got.reshape(-1)].astype(jnp.float32) + group_ctx[local_user]
    rows_in = jnp.where(live_slot, rms_round(rebuilt), jnp.zeros((), jnp.bfloat16))
    pieces = sent_together((w_gate[0], w_up[0]), DP, 0, 1)
    columns = rows_in
    gate_pre = jnp.dot(columns, pieces[0], preferred_element_type=jnp.float32)
    up_pre = jnp.dot(columns, pieces[1], preferred_element_type=jnp.float32)
    silu_val, silu_grad = silu_pair(gate_pre)
    hidden = (silu_val * up_pre).astype(jnp.bfloat16)
    expert_out = jnp.dot(
        hidden, whole_of(w_down[0], DP, 1), preferred_element_type=jnp.float32
    ).astype(jnp.bfloat16)
    returned = lax.all_to_all(
        expert_out.reshape(expert_devs, capacity, model_width),
        EXPERT,
        split_axis=0,
        concat_axis=0,
        tiled=True,
    )
    mixed_in = returned.reshape(experts * capacity, model_width)[slot_dest].reshape(
        row_total, 2, model_width
    )
    moe_sum = mix[:, 0:1] * mixed_in[:, 0].astype(jnp.float32) + mix[:, 1:2] * mixed_in[
        :, 1
    ].astype(jnp.float32)
    h_rows = (x_sum.reshape(row_total, model_width) + moe_sum).reshape(
        user_count, CANDS, model_width
    )
    inv_rms = lax.rsqrt(jnp.mean(h_rows * h_rows, axis=-1, keepdims=True) + norm_eps)
    unit_rows = h_rows * inv_rms
    scored = unit_rows * out_gain
    query_f = user_query.astype(jnp.float32)
    listwise = jnp.einsum(
        "ucd,ud->uc", scored, query_f, precision=lax.Precision.HIGHEST
    ) / math.sqrt(D)
    top_list = jnp.max(listwise, axis=-1, keepdims=True)
    expo = jnp.exp(listwise - top_list)
    expo_total = jnp.sum(expo, axis=-1, keepdims=True)
    losses = jnp.log(expo_total[:, 0]) + top_list[:, 0] - listwise[:, 0]
    first_one = (jnp.arange(CANDS, dtype=jnp.int32) == 0).astype(jnp.float32)[None, :]
    d_list = loss_scale * (expo / expo_total - first_one)
    d_scored = d_list[..., None] * query_f[:, None, :] / math.sqrt(D)
    d_unit = d_scored * out_gain
    d_h = inv_rms * (d_unit - unit_rows * jnp.mean(d_unit * unit_rows, axis=-1, keepdims=True))
    d_h = d_h.reshape(row_total, model_width)
    d_out = (mix[:, :, None] * d_h[:, None, :]).astype(jnp.bfloat16)
    d_mix = jnp.sum(d_h[:, None, :] * mixed_in.astype(jnp.float32), axis=-1)
    mix_dot = jnp.sum(mix * d_mix, axis=1, keepdims=True)
    d_aff = (d_mix - mix_dot) / aff_total
    d_pick = d_aff * affinity * (1.0 - affinity)
    route_hot = (routes[:, :, None] == jnp.arange(experts, dtype=jnp.int32)).astype(jnp.float32)
    d_logits = jnp.sum(route_hot * d_pick[:, :, None], axis=1).astype(jnp.bfloat16)
    contract_rows = (((0,), (0,)), ((), ()))
    router_term = lax.dot_general(
        normed, d_logits, contract_rows, preferred_element_type=jnp.float32
    )
    grad_send = (
        jnp.zeros((experts * capacity, model_width), jnp.bfloat16)
        .at[slot_dest]
        .set(d_out.reshape(-1, model_width))
    )
    grad_rows = lax.all_to_all(
        grad_send.reshape(experts, capacity, model_width),
        EXPERT,
        split_axis=0,
        concat_axis=0,
        tiled=True,
    ).reshape(slot_count, model_width)
    contract_cols = (((1,), (1,)), ((), ()))
    columns = grad_rows
    d_hidden = lax.dot_general(
        columns, whole_of(w_down[0], DP, 1), contract_cols, preferred_element_type=jnp.float32
    )
    d_gate = (d_hidden * up_pre * silu_grad).astype(jnp.bfloat16)
    d_up = (d_hidden * silu_val).astype(jnp.bfloat16)
    summed = lax.psum_scatter(
        jnp.concatenate(
            [
                lax.dot_general(rows_in, d_gate, contract_rows, preferred_element_type=jnp.float32),
                lax.dot_general(rows_in, d_up, contract_rows, preferred_element_type=jnp.float32),
                lax.dot_general(
                    grad_rows, hidden, contract_rows, preferred_element_type=jnp.float32
                ),
            ],
            axis=1,
        ).astype(jnp.bfloat16),
        DP,
        scatter_dimension=0,
        tiled=True,
    ).astype(jnp.float32)
    grad_gate = summed[:, :FF][None]
    grad_up = summed[:, FF : 2 * FF][None]
    grad_down = summed[:, 2 * FF :].T[None]
    grad_router = over_axes_2(router_term, DP_EXPERT)
    return (losses, grad_gate, grad_up, grad_down, grad_router)


def solution(mesh):
    torus = Mesh(mesh.devices.reshape(8, 2, 4, 4), ("dp_0", "dp_1", "expert_0", "expert_1"))
    return jax.shard_map(
        local,
        mesh=torus,
        in_specs=(
            P(DP_EXPERT, None, None),
            P(DP_EXPERT),
            P(DP_EXPERT, None),
            P(DP_EXPERT, None),
            P(DP_EXPERT, None),
            P(DP_EXPERT, None),
            P(),
            P(EXPERT, DP, None),
            P(EXPERT, DP, None),
            P(EXPERT, None, DP),
            P(),
        ),
        out_specs=(
            P(DP_EXPERT),
            P(EXPERT, DP, None),
            P(EXPERT, DP, None),
            P(EXPERT, None, DP),
            P(),
        ),
        check_vma=False,
    )
```

profile of v0, /device:TPU:2, one launch (start us, length us, event | category | flops | bytes accessed | tf_op | source)
XLA Modules:
  0.0 581.2 jit_solution(2815404170481698003)
XLA Ops:
  15.3 7.5 %all-to-all-start = ((s32[16,1,32]{2,1,0:T(1,128)}), s32[16,1,32]{2,1,0:T(1,128)S(1)}, u32[]{:S(2)}, u32[]{:S(2)}) async-start(s32[16,1,32]{2,1,0:T(1,128)} %all_to_all.18), calls=%async_computation | async-start | bytes 16384 | tf_op jit(solution)/shard_map/all_to_all | solution.py:112
  22.8 3.7 all-gather
  26.6 5.7 fusion.2
  32.5 5.1 fusion.4
  37.9 23.4 %all-gather.3 = f32[16,2,2048]{2,1,0:T(2,128)S(1)} all-gather(f32[1,2,2048]{2,1,0:T(2,128)S(1)} %reshape.537), channel_id=1, replica_groups=mesh['dp_0'=8,'dp_1'=2,'expert_0'=4,'expert_1'=4] {'expert_0','expert_1'}, dimensions={0}, use_global_device_ids=true | all-gather | bytes 278528 | tf_op jit(solution)/shard_map/all_gather | solution.py:116
  66.5 6.3 %all-to-all-start.1 = ((s32[16,1,32]{2,1,0:T(1,128)}), s32[16,1,32]{2,1,0:T(1,128)S(1)}, u32[]{:S(2)}, u32[]{:S(2)}) async-start(s32[16,1,32]{2,1,0:T(1,128)} %all_to_all.20), calls=%async_computation.1 | async-start | bytes 16384 | tf_op jit(solution)/shard_map/all_to_all | solution.py:109
  72.9 5.9 %all-to-all-done.1 = s32[16,1,32]{2,1,0:T(1,128)S(1)} async-done(((s32[16,1,32]{2,1,0:T(1,128)}), s32[16,1,32]{2,1,0:T(1,128)S(1)}, u32[]{:S(2)}, u32[]{:S(2)}) %all-to-all-start.1) | async-done | bytes 2080 | tf_op jit(solution)/shard_map/all_to_all | solution.py:109
  80.2 3.7 gather_fusion.2
  83.8 34.7 %all-gather.12.cloned.1.call-done = bf16[256,2,2048]{2,1,0:T(2,128)(2,1)} async-done(((bf16[1,2,2048]{2,1,0:T(2,128)(2,1)}), bf16[256,2,2048]{2,1,0:T(2,128)(2,1)}) %all-gather.12.cloned.1.call-update) | async-done | bytes 2097168 | tf_op jit(solution)/shard_map/all_gather | solution.py:84
  121.3 3.3 gather_fusion.1
  124.6 3.6 multiply_reduce_fusion
  131.3 34.9 %all-gather.8.cloned.1.call-done = bf16[2048,1536]{1,0:T(8,128)(2,1)} async-done(((bf16[128,1536]{1,0:T(8,128)(2,1)}), bf16[2048,1536]{1,0:T(8,128)(2,1)}) %all-gather.8.cloned.1.call-update) | async-done | bytes 6291472 | tf_op jit(solution)/shard_map/all_gather | solution.py:23
  166.2 4.5 fusion.10
  171.9 3.0 multiply_convert_fusion.4
  174.8 46.7 %all-gather.10.cloned.1.call-done = bf16[1,768,2048]{2,1,0:T(8,128)(2,1)} async-done(((bf16[1,768,256]{2,1,0:T(8,128)(2,1)}), bf16[1,768,2048]{2,1,0:T(8,128)(2,1)}) %all-gather.10.cloned.1.call-update) | async-done | bytes 3145744 | tf_op jit(solution)/shard_map/all_gather | solution.py:30
  221.5 5.1 fusion.16
  226.6 7.7 %all-to-all-start.2 = ((bf16[16,32,2048]{2,1,0:T(8,128)(2,1)}), bf16[16,32,2048]{2,1,0:T(8,128)(2,1)}, u32[]{:S(2)}, u32[]{:S(2)}) async-start(bf16[16,32,2048]{2,1,0:T(8,128)(2,1)} %bitcast.109), calls=%async_computation.2 | async-start | bytes 4194304 | tf_op jit(solution)/shard_map/all_to_all | solution.py:131
  239.3 18.4 %all-to-all-done.2 = bf16[16,32,2048]{2,1,0:T(8,128)(2,1)} async-done(((bf16[16,32,2048]{2,1,0:T(8,128)(2,1)}), bf16[16,32,2048]{2,1,0:T(8,128)(2,1)}, u32[]{:S(2)}, u32[]{:S(2)}) %all-to-all-start.2) | async-done | bytes 2097184 | tf_op jit(solution)/shard_map/all_to_all | solution.py:131
  257.6 4.2 gather_fusion.3
  265.4 3.4 multiply_reduce_fusion.3
  280.2 3.8 mul.323
  284.1 4.9 scatter_custom_fusion.2
  288.9 5.9 %all-to-all-start.3 = ((bf16[16,32,2048]{2,1,0:T(8,128)(2,1)}), bf16[16,32,2048]{2,1,0:T(8,128)(2,1)}, u32[]{:S(2)}, u32[]{:S(2)}) async-start(bf16[16,32,2048]{2,1,0:T(8,128)(2,1)} %bitcast.108), calls=%async_computation.3 | async-start | bytes 4194304 | tf_op jit(solution)/shard_map/all_to_all | solution.py:180
  297.1 72.1 %all-reduce.5.cloned.1.call-done = f32[2048,16]{0,1:T(8,128)} async-done(((f32[2048,16]{0,1:T(8,128)}), f32[2048,16]{0,1:T(8,128)}) %all-reduce.5.cloned.1.call-update) | async-done | bytes 131088 | tf_op jit(solution)/shard_map/psum | solution.py:36
  369.3 29.7 %all-reduce.7.cloned.1.call-done = f32[2048,16]{0,1:T(8,128)} async-done(((f32[2048,16]{0,1:T(8,128)}), f32[2048,16]{0,1:T(8,128)}) %all-reduce.7.cloned.1.call-update) | async-done | bytes 131088 | tf_op jit(solution)/shard_map/psum | solution.py:36
  399.1 3.8 convolution_convert_fusion
  402.9 3.6 fusion.12
  410.5 4.4 pad_maximum_fusion
  414.9 12.2 %copy.109 = bf16[2048,2304]{1,0:T(8,128)(2,1)} copy(bf16[2048,2304]{0,1:T(8,128)(2,1)} %pad_maximum_fusion) | data formatting | bytes 18874368
  427.8 20.0 %all-reduce.9.cloned.1.call-done = f32[2048,16]{0,1:T(8,128)} async-done(((f32[2048,16]{0,1:T(8,128)}), f32[2048,16]{0,1:T(8,128)}) %all-reduce.9.cloned.1.call-update) | async-done | bytes 131088 | tf_op jit(solution)/shard_map/psum | solution.py:36
  447.8 76.7 %reduce-scatter.4.cloned.1.call-done = bf16[128,2304]{1,0:T(8,128)(2,1)} async-done(((bf16[2048,2304]{1,0:T(8,128)(2,1)}), bf16[128,2304]{1,0:T(8,128)(2,1)}) %reduce-scatter.4.cloned.1.call-update) | async-done | bytes 589840
  528.6 43.9 %all-reduce.11.cloned.1.call-done = f32[2048,16]{0,1:T(8,128)} async-done(((f32[2048,16]{0,1:T(8,128)}), f32[2048,16]{0,1:T(8,128)}) %all-reduce.11.cloned.1.call-update) | async-done | bytes 131088 | tf_op jit(solution)/shard_map/psum | solution.py:36
  (173 shorter events, 54.7 us)
Async XLA Ops:
  7.2 229.1 %copy-start = (bf16[2048,16]{0,1:T(8,128)(2,1)S(1)}, bf16[2048,16]{0,1:T(8,128)(2,1)}, u32[]{:S(2)}) copy-start(bf16[2048,16]{0,1:T(8,128)(2,1)} %param.17) | copy-start | bytes 196612
  7.2 19.3 %copy-start.16 = (s32[2]{0:T(128)S(1)}, s32[2]{0:T(128)}, u32[]{:S(2)}) copy-start(s32[2]{0:T(128)} %param.12) | copy-start | bytes 28
  7.2 19.4 %copy-start.11 = (bf16[2,2048]{1,0:T(2,128)(2,1)S(1)}, bf16[2,2048]{1,0:T(2,128)(2,1)}, u32[]{:S(2)}) copy-start(bf16[2,2048]{1,0:T(2,128)(2,1)} %param.13) | copy-start | bytes 24580
  7.2 111.3 %all-gather.12.cloned.1.call-start = ((), (), s32[]{:S(2)}) async-start(), calls=%async_computation.11 | async-start | bytes 2105344 | tf_op jit(solution)/shard_map/all_gather | solution.py:84
  7.9 158.3 %all-gather.8.cloned.1.call-start = ((), (), s32[]{:S(2)}) async-start(), calls=%async_computation.5 | async-start | bytes 6684672 | tf_op jit(solution)/shard_map/all_gather | solution.py:23
  15.3 51.2 %all-to-all-start = ((s32[16,1,32]{2,1,0:T(1,128)}), s32[16,1,32]{2,1,0:T(1,128)S(1)}, u32[]{:S(2)}, u32[]{:S(2)}) async-start(s32[16,1,32]{2,1,0:T(1,128)} %all_to_all.18), calls=%async_computation | async-start | bytes 16384 | tf_op jit(solution)/shard_map/all_to_all | solution.py:112
  22.7 198.8 %all-gather.10.cloned.1.call-start = ((), (), s32[]{:S(2)}) async-start(), calls=%async_computation.10 | async-start | bytes 3538944 | tf_op jit(solution)/shard_map/all_gather | solution.py:30
  32.5 5.1 copy-start.15
  32.5 5.3 copy-start.13
  32.5 31.3 %copy-start.12 = (bf16[2,2048]{1,0:T(2,128)(2,1)S(1)}, bf16[2,2048]{1,0:T(2,128)(2,1)}, u32[]{:S(2)}) copy-start(bf16[2,2048]{1,0:T(2,128)(2,1)} %param.14) | copy-start | bytes 24580
  66.5 12.3 %all-to-all-start.1 = ((s32[16,1,32]{2,1,0:T(1,128)}), s32[16,1,32]{2,1,0:T(1,128)S(1)}, u32[]{:S(2)}, u32[]{:S(2)}) async-start(s32[16,1,32]{2,1,0:T(1,128)} %all_to_all.20), calls=%async_computation.1 | async-start | bytes 16384 | tf_op jit(solution)/shard_map/all_to_all | solution.py:109
  124.6 4.1 copy-start.2
  124.6 4.7 copy-start.3
  166.2 5.6 copy-start.7
  166.2 5.6 copy-start.17
  174.8 51.7 %copy-start.21 = (bf16[512,768]{1,0:T(8,128)(2,1)}, bf16[512,768]{1,0:T(8,128)(2,1)S(1)}, u32[]{:S(2)}) copy-start(bf16[512,768]{1,0:T(8,128)(2,1)S(1)} %get-tuple-element.59) | copy-start | bytes 2359300
  226.6 7.7 %copy-start.14 = (f32[2048]{0:T(1024)S(1)}, f32[2048]{0:T(1024)}, u32[]{:S(2)}) copy-start(f32[2048]{0:T(1024)} %param.21) | copy-start | bytes 24580
  226.6 31.1 %all-to-all-start.2 = ((bf16[16,32,2048]{2,1,0:T(8,128)(2,1)}), bf16[16,32,2048]{2,1,0:T(8,128)(2,1)}, u32[]{:S(2)}, u32[]{:S(2)}) async-start(bf16[16,32,2048]{2,1,0:T(8,128)(2,1)} %bitcast.109), calls=%async_computation.2 | async-start | bytes 4194304 | tf_op jit(solution)/shard_map/all_to_all | solution.py:131
  236.3 2.2 copy-start.4
  269.0 3.3 copy-start.10
  270.6 3.2 copy-start.6
  288.9 110.2 %all-to-all-start.3 = ((bf16[16,32,2048]{2,1,0:T(8,128)(2,1)}), bf16[16,32,2048]{2,1,0:T(8,128)(2,1)}, u32[]{:S(2)}, u32[]{:S(2)}) async-start(bf16[16,32,2048]{2,1,0:T(8,128)(2,1)} %bitcast.108), calls=%async_computation.3 | async-start | bytes 4194304 | tf_op jit(solution)/shard_map/all_to_all | solution.py:180
  294.9 74.4 %all-reduce.5.cloned.1.call-start = ((), (), s32[]{:S(2)}) async-start(), calls=%async_computation.6 | async-start | bytes 262144 | tf_op jit(solution)/shard_map/psum | solution.py:36
  297.1 101.9 %all-reduce.7.cloned.1.call-start = ((), (), s32[]{:S(2)}) async-start(), calls=%async_computation.7 | async-start | bytes 262144 | tf_op jit(solution)/shard_map/psum | solution.py:36
  369.3 78.5 %all-reduce.9.cloned.1.call-start = ((), (), s32[]{:S(2)}) async-start(), calls=%async_computation.8 | async-start | bytes 262144 | tf_op jit(solution)/shard_map/psum | solution.py:36
  399.1 125.4 %reduce-scatter.4.cloned.1.call-start = ((), (), s32[]{:S(2)}) async-start(), calls=%async_computation.12 | async-start | bytes 10027008
  399.1 3.8 copy-start.18
  402.9 3.6 copy-start.8
  402.9 3.6 copy-start.20
  406.5 1.9 copy-start.22
  427.1 145.4 %all-reduce.11.cloned.1.call-start = ((), (), s32[]{:S(2)}) async-start(), calls=%async_computation.9 | async-start | bytes 262144 | tf_op jit(solution)/shard_map/psum | solution.py:36
  525.9 48.2 %copy-start.1 = (bf16[2048,16]{0,1:T(8,128)(2,1)S(1)}, bf16[2048,16]{0,1:T(8,128)(2,1)}, u32[]{:S(2)}) copy-start(bf16[2048,16]{0,1:T(8,128)(2,1)} %param.17) | copy-start | bytes 196612
  (3 other events, 3.3 us)
Sparse Core Ops, SparseCore 0:
  11.8 106.7 all-gather.11
  120.9 45.2 all-gather.7
  168.0 53.5 all-gather.9
  298.3 70.9 all-reduce.4
  371.8 27.1 all-reduce.6
  401.3 46.4 all-reduce.8
  450.3 74.1 reduce-scatter.3
  526.8 45.6 all-reduce.10
where the time goes:
time: 589 us; the launch traced here: 581 us
  waiting for transfers between devices  384 us (65%)
  local copies, waits for them, and re-layouts  59.2 us (10%)
  matrix products  36.6 us (6%)
  other arithmetic  31.9 us (5%)
  starting transfers between devices  27.7 us (5%)
  blocking collectives  27.1 us (5%)
  between operations  15 us (3%)
    psum x4, waiting for transfers between devices, over_axes_2(): x = lax.psum(x, axis)  166 us
    unnamed x9, waiting for transfers between devices  77.5 us
    all_gather x1, waiting for transfers between devices, whole_of(): result = lax.all_gather(result, axes[number], axis=dim, tiled=True)  46.7 us
    all_gather x1, waiting for transfers between devices, sent_together(): result = lax.all_gather(both, axis, axis=dim, tiled=True)  34.9 us
    all_gather x1, waiting for transfers between devices, local(): all_items = lax.all_gather(pos_item, DP_EXPERT, axis=0, tiled=True)  34.7 us
    unnamed x59, local copies, waits for them, and re-layouts  26.9 us
    all_gather x1, blocking collectives, local(): group_ctx = lax.all_gather(context, EXPERT, axis=0, tiled=True)  23.4 us
    all_to_all x1, waiting for transfers between devices, local(): lax.all_to_all(expert_out.reshape(expert_devs, capacity, model_width), EX...  18.4 us
  transfers between devices with their start and end apart: 12, of which 10 were waited for; matrix products, arithmetic and copies ran while one was open for 15% of the time, Pallas kernels for 0%

commit v1 on v0

--- a/solution.py
+++ b/solution.py
@@ -81,7 +81,9 @@
     context = jnp.einsum(
         "uht,uthd->uhd", attn_probs, key_heads, preferred_element_type=jnp.float32
     ).reshape(user_count, model_width)
-    all_items = lax.all_gather(pos_item, DP_EXPERT, axis=0, tiled=True)
+    all_items = jnp.concatenate(
+        lax.all_to_all(jnp.stack([pos_item] * lax.axis_size(DP_EXPERT)), DP_EXPERT, 0, 0), axis=0
+    )
     candidates = jnp.concatenate([pos_item[:, None, :], all_items[neg_index]], axis=1)
     x_sum = candidates.astype(jnp.float32) + context[:, None, :]
     normed = rms_round(x_sum).reshape(row_total, model_width)

time: 589 us -> 512 us (0.87)
  waiting for transfers between devices: 384 us -> 284 us
  blocking collectives: 27.1 us -> 37.6 us
  starting transfers between devices: 27.7 us -> 35.2 us
    all_gather x1, waiting for transfers between devices: 46.7 us -> 8.04 us  [whole_of(): result = lax.all_gather(result, axes[number], axis=dim, tiled=True)]
    all_gather x1, waiting for transfers between devices: 34.9 us -> 0.01 us  [sent_together(): result = lax.all_gather(both, axis, axis=dim, tiled=True)]
    all_gather x1 -> x0, waiting for transfers between devices: 34.7 us -> none  [local(): all_items = lax.all_gather(pos_item, DP_EXPERT, axis=0, tiled=True)]
    all_to_all x0 -> x1, blocking collectives: none -> 10.5 us  [local(): lax.all_to_all(item_send.reshape(experts, capacity), EXPERT, split_axis=0...]
    all_to_all x1, starting transfers between devices: 6.26 us -> 12.8 us  [local(): lax.all_to_all(jnp.stack([pos_item] * lax.axis_size(DP_EXPERT)), DP_EXPER...]
    unnamed x59 -> x60, local copies, waits for them, and re-layouts: 26.9 us -> 24.2 us
    unnamed x9 -> x8, waiting for transfers between devices: 77.5 us -> 76.7 us
  transfers between devices with their start and end apart: 12 -> 11, of which waited for: 10 -> 9; matrix products, arithmetic and copies ran while one was open for 15% -> 17% of each run, Pallas kernels for 0% -> 0%
where the time goes in v1:
time: 512 us; the launch traced here: 503 us
  waiting for transfers between devices  284 us (55%)
  local copies, waits for them, and re-layouts  61.8 us (12%)
  blocking collectives  37.6 us (7%)
  matrix products  36.7 us (7%)
  starting transfers between devices  35.2 us (7%)
  other arithmetic  32.7 us (6%)
  between operations  15 us (3%)
    psum x4, waiting for transfers between devices, over_axes_2(): x = lax.psum(x, axis)  165 us
    unnamed x8, waiting for transfers between devices  76.7 us
    all_gather x1, blocking collectives, local(): group_ctx = lax.all_gather(context, EXPERT, axis=0, tiled=True)  24.7 us
    unnamed x60, local copies, waits for them, and re-layouts  24.2 us
    all_to_all x1, waiting for transfers between devices, local(): lax.all_to_all(expert_out.reshape(expert_devs, capacity, model_width), EX...  20.1 us
    all_to_all x1, starting transfers between devices, local(): lax.all_to_all(jnp.stack([pos_item] * lax.axis_size(DP_EXPERT)), DP_EXPER...  12.8 us
    all_to_all x1, waiting for transfers between devices, local(): lax.all_to_all(jnp.stack([pos_item] * lax.axis_size(DP_EXPERT)), DP_EXPER...  10.6 us
    all_to_all x1, blocking collectives, local(): lax.all_to_all(item_send.reshape(experts, capacity), EXPERT, split_axis=0...  10.5 us
  transfers between devices with their start and end apart: 11, of which 9 were waited for; matrix products, arithmetic and copies ran while one was open for 17% of the time, Pallas kernels for 0%

profile of v1, /device:TPU:2, one launch (start us, length us, event | category | flops | bytes accessed | tf_op | source)
XLA Modules:
  0.0 503.3 jit_solution(12296068058131228668)
XLA Ops:
  14.5 7.5 %all-to-all-start.1 = ((s32[16,1,32]{2,1,0:T(1,128)}), s32[16,1,32]{2,1,0:T(1,128)S(1)}, u32[]{:S(2)}, u32[]{:S(2)}) async-start(s32[16,1,32]{2,1,0:T(1,128)} %all_to_all.22), calls=%async_computation.1 | async-start | bytes 16384 | tf_op jit(solution)/shard_map/all_to_all | solution.py:114
  24.5 3.5 all-to-all-done.1
  28.1 10.5 %all_to_all.33 = s32[16,1,32]{2,1,0:T(1,128)S(1)} all-to-all(s32[16,1,32]{2,1,0:T(1,128)S(1)} %all_to_all.24), channel_id=1, replica_groups=mesh['dp_0'=8,'dp_1'=2,'expert_0'=4,'expert_1'=4] {'expert_0','expert_1'}, dimensions={0} | all-to-all | bytes 4096 | tf_op jit(solution)/shard_map/all_to_all | solution.py:111
  38.6 3.1 stack.2
  41.7 12.8 %all-to-all-start = ((bf16[256,2,2048]{2,1,0:T(2,128)(2,1)}), bf16[256,2,2048]{2,1,0:T(2,128)(2,1)}, u32[]{:S(2)}, u32[]{:S(2)}) async-start(bf16[256,2,2048]{2,1,0:T(2,128)(2,1)} %stack.2), calls=%async_computation | async-start | bytes 4194304 | tf_op jit(solution)/shard_map/all_to_all | solution.py:85
  57.1 5.7 %fusion.2 = f32[2,16,1,1024]{3,2,1,0:T(1,128)S(1)} fusion(bf16[2,16,128,1]{2,3,1,0:T(2,128)(2,1)S(1)} %reshape.551, bf16[2,1024,2048]{2,1,0:T(8,128)(2,1)} %param.11), kind=kOutput, calls=%fused_computation.11 | convolution fusion | flops 8388608 | bytes 8527872 | tf_op jit(solution)/shard_map/uhd,uthd->uht/dot_general | solution.py:73
  63.0 5.1 %fusion.4 = f32[2,16,1,128]{3,2,1,0:T(1,128)S(1)} fusion(bf16[2,16,1024,1]{2,1,0,3:T(8,128)(2,1)S(1)} %fusion.26, bf16[2,1024,2048]{2,1,0:T(8,128)(2,1)} %param.11), kind=kOutput, calls=%fused_computation.13 | convolution fusion | flops 8388608 | bytes 8470528 | tf_op jit(solution)/shard_map/uht,uthd->uhd/dot_general | solution.py:81
  68.1 24.7 %all-gather.2 = f32[16,2,2048]{2,1,0:T(2,128)S(1)} all-gather(f32[1,2,2048]{2,1,0:T(2,128)S(1)} %reshape.541), channel_id=1, replica_groups=mesh['dp_0'=8,'dp_1'=2,'expert_0'=4,'expert_1'=4] {'expert_0','expert_1'}, dimensions={0}, use_global_device_ids=true | all-gather | bytes 278528 | tf_op jit(solution)/shard_map/all_gather | solution.py:118
  97.4 3.7 gather_fusion.2
  101.1 10.6 %all-to-all-done = bf16[256,2,2048]{2,1,0:T(2,128)(2,1)} async-done(((bf16[256,2,2048]{2,1,0:T(2,128)(2,1)}), bf16[256,2,2048]{2,1,0:T(2,128)(2,1)}, u32[]{:S(2)}, u32[]{:S(2)}) %all-to-all-start) | async-done | bytes 2097184 | tf_op jit(solution)/shard_map/all_to_all | solution.py:85
  114.5 3.3 gather_fusion.1
  117.8 3.7 multiply_reduce_fusion
  124.6 4.5 fusion.10
  130.3 3.0 multiply_convert_fusion.4
  133.3 8.0 %all-gather.8.cloned.1.call-done = bf16[1,768,2048]{2,1,0:T(8,128)(2,1)} async-done(((bf16[1,768,256]{2,1,0:T(8,128)(2,1)}), bf16[1,768,2048]{2,1,0:T(8,128)(2,1)}) %all-gather.8.cloned.1.call-update) | async-done | bytes 3145744 | tf_op jit(solution)/shard_map/all_gather | solution.py:30
  141.4 5.1 %fusion.16 = bf16[512,2048]{1,0:T(8,128)(2,1)} fusion(bf16[512,768]{1,0:T(8,128)(2,1)S(1)} %get-tuple-element.59, bf16[1,768,2048]{2,1,0:T(8,128)(2,1)} %all-gather.8.cloned.1.call-done), kind=kOutput, calls=%fused_computation.31 | convolution fusion | flops 1611661312 | bytes 6029312 | tf_op jit(solution)/shard_map/dot_general | solution.py:130
  146.4 7.7 %all-to-all-start.3 = ((bf16[16,32,2048]{2,1,0:T(8,128)(2,1)}), bf16[16,32,2048]{2,1,0:T(8,128)(2,1)}, u32[]{:S(2)}, u32[]{:S(2)}) async-start(bf16[16,32,2048]{2,1,0:T(8,128)(2,1)} %bitcast.108), calls=%async_computation.3 | async-start | bytes 4194304 | tf_op jit(solution)/shard_map/all_to_all | solution.py:133
  159.1 20.1 %all-to-all-done.3 = bf16[16,32,2048]{2,1,0:T(8,128)(2,1)} async-done(((bf16[16,32,2048]{2,1,0:T(8,128)(2,1)}), bf16[16,32,2048]{2,1,0:T(8,128)(2,1)}, u32[]{:S(2)}, u32[]{:S(2)}) %all-to-all-start.3) | async-done | bytes 2097184 | tf_op jit(solution)/shard_map/all_to_all | solution.py:133
  179.2 4.2 gather_fusion.3
  187.0 3.4 multiply_reduce_fusion.3
  201.8 3.8 mul.323
  205.7 4.9 scatter_custom_fusion.2
  210.5 7.0 %all-to-all-start.4 = ((bf16[16,32,2048]{2,1,0:T(8,128)(2,1)}), bf16[16,32,2048]{2,1,0:T(8,128)(2,1)}, u32[]{:S(2)}, u32[]{:S(2)}) async-start(bf16[16,32,2048]{2,1,0:T(8,128)(2,1)} %bitcast.107), calls=%async_computation.4 | async-start | bytes 4194304 | tf_op jit(solution)/shard_map/all_to_all | solution.py:182
  219.8 71.6 %all-reduce.5.cloned.1.call-done = f32[2048,16]{0,1:T(8,128)} async-done(((f32[2048,16]{0,1:T(8,128)}), f32[2048,16]{0,1:T(8,128)}) %all-reduce.5.cloned.1.call-update) | async-done | bytes 131088 | tf_op jit(solution)/shard_map/psum | solution.py:36
  291.5 29.7 %all-reduce.7.cloned.1.call-done = f32[2048,16]{0,1:T(8,128)} async-done(((f32[2048,16]{0,1:T(8,128)}), f32[2048,16]{0,1:T(8,128)}) %all-reduce.7.cloned.1.call-update) | async-done | bytes 131088 | tf_op jit(solution)/shard_map/psum | solution.py:36
  321.3 3.8 convolution_convert_fusion
  325.1 3.6 fusion.12
  332.7 4.4 pad_maximum_fusion
  337.1 12.2 %copy.109 = bf16[2048,2304]{1,0:T(8,128)(2,1)} copy(bf16[2048,2304]{0,1:T(8,128)(2,1)} %pad_maximum_fusion) | data formatting | bytes 18874368
  350.0 19.9 %all-reduce.9.cloned.1.call-done = f32[2048,16]{0,1:T(8,128)} async-done(((f32[2048,16]{0,1:T(8,128)}), f32[2048,16]{0,1:T(8,128)}) %all-reduce.9.cloned.1.call-update) | async-done | bytes 131088 | tf_op jit(solution)/shard_map/psum | solution.py:36
  370.0 76.6 %reduce-scatter.4.cloned.1.call-done = bf16[128,2304]{1,0:T(8,128)(2,1)} async-done(((bf16[2048,2304]{1,0:T(8,128)(2,1)}), bf16[128,2304]{1,0:T(8,128)(2,1)}) %reduce-scatter.4.cloned.1.call-update) | async-done | bytes 589840
  450.6 44.0 %all-reduce.11.cloned.1.call-done = f32[2048,16]{0,1:T(8,128)} async-done(((f32[2048,16]{0,1:T(8,128)}), f32[2048,16]{0,1:T(8,128)}) %all-reduce.11.cloned.1.call-update) | async-done | bytes 131088 | tf_op jit(solution)/shard_map/psum | solution.py:36
  (174 shorter events, 56.5 us)
Async XLA Ops:
  7.2 149.0 %copy-start = (bf16[2048,16]{0,1:T(8,128)(2,1)S(1)}, bf16[2048,16]{0,1:T(8,128)(2,1)}, u32[]{:S(2)}) copy-start(bf16[2048,16]{0,1:T(8,128)(2,1)} %param.17) | copy-start | bytes 196612
  7.2 117.4 %all-gather.6.cloned.1.call-start = ((), (), s32[]{:S(2)}) async-start(), calls=%async_computation.6 | async-start | bytes 6684672 | tf_op jit(solution)/shard_map/all_gather | solution.py:23
  14.5 13.6 %all-to-all-start.1 = ((s32[16,1,32]{2,1,0:T(1,128)}), s32[16,1,32]{2,1,0:T(1,128)S(1)}, u32[]{:S(2)}, u32[]{:S(2)}) async-start(s32[16,1,32]{2,1,0:T(1,128)} %all_to_all.22), calls=%async_computation.1 | async-start | bytes 16384 | tf_op jit(solution)/shard_map/all_to_all | solution.py:114
  41.7 12.8 %copy-start.11 = (bf16[1,768,128]{2,1,0:T(8,128)(2,1)S(1)}, bf16[1,768,128]{2,1,0:T(8,128)(2,1)}, u32[]{:S(2)}) copy-start(bf16[1,768,128]{2,1,0:T(8,128)(2,1)} %param.20) | copy-start | bytes 589828
  41.7 15.2 %copy-start.13 = (bf16[2,2048]{1,0:T(2,128)(2,1)S(1)}, bf16[2,2048]{1,0:T(2,128)(2,1)}, u32[]{:S(2)}) copy-start(bf16[2,2048]{1,0:T(2,128)(2,1)} %param.13) | copy-start | bytes 24580
  41.7 15.3 %copy-start.17 = (s32[2]{0:T(128)S(1)}, s32[2]{0:T(128)}, u32[]{:S(2)}) copy-start(s32[2]{0:T(128)} %param.12) | copy-start | bytes 28
  41.7 70.0 %all-to-all-start = ((bf16[256,2,2048]{2,1,0:T(2,128)(2,1)}), bf16[256,2,2048]{2,1,0:T(2,128)(2,1)}, u32[]{:S(2)}, u32[]{:S(2)}) async-start(bf16[256,2,2048]{2,1,0:T(2,128)(2,1)} %stack.2), calls=%async_computation | async-start | bytes 4194304 | tf_op jit(solution)/shard_map/all_to_all | solution.py:85
  54.5 86.8 %all-gather.8.cloned.1.call-start = ((), (), s32[]{:S(2)}) async-start(), calls=%async_computation.11 | async-start | bytes 3538944 | tf_op jit(solution)/shard_map/all_gather | solution.py:30
  63.0 30.1 %copy-start.16 = (s32[2,63]{1,0:T(2,128)S(1)}, s32[2,63]{1,0:T(2,128)}, u32[]{:S(2)}) copy-start(s32[2,63]{1,0:T(2,128)} %param.15) | copy-start | bytes 1516
  63.0 30.2 %copy-start.12 = (bf16[2,2048]{1,0:T(2,128)(2,1)S(1)}, bf16[2,2048]{1,0:T(2,128)(2,1)}, u32[]{:S(2)}) copy-start(bf16[2,2048]{1,0:T(2,128)(2,1)} %param.14) | copy-start | bytes 24580
  63.0 30.2 %copy-start.14 = (s32[128,2]{0,1:T(2,128)S(1)}, s32[128,2]{0,1:T(2,128)}, u32[]{:S(2)}) copy-start(s32[128,2]{0,1:T(2,128)} %param.16) | copy-start | bytes 3076
  117.8 4.2 copy-start.2
  117.8 4.9 copy-start.3
  124.6 5.7 %copy-start.7 = (bf16[512,2048]{1,0:T(8,128)(2,1)S(1)}, bf16[512,2048]{1,0:T(8,128)(2,1)}, u32[]{:S(2)}) copy-start(bf16[512,2048]{1,0:T(8,128)(2,1)} %fusion.19) | copy-start | bytes 6291460
  124.6 5.7 %copy-start.18 = (bf16[2048,1536]{1,0:T(8,128)(2,1)S(1)}, bf16[2048,1536]{1,0:T(8,128)(2,1)}, u32[]{:S(2)}) copy-start(bf16[2048,1536]{1,0:T(8,128)(2,1)} %all-gather.6.cloned.1.call-done) | copy-start | bytes 18874372
  133.3 13.1 %copy-start.22 = (bf16[512,768]{1,0:T(8,128)(2,1)}, bf16[512,768]{1,0:T(8,128)(2,1)S(1)}, u32[]{:S(2)}) copy-start(bf16[512,768]{1,0:T(8,128)(2,1)S(1)} %get-tuple-element.59) | copy-start | bytes 2359300
  146.4 7.7 %copy-start.15 = (f32[2048]{0:T(1024)S(1)}, f32[2048]{0:T(1024)}, u32[]{:S(2)}) copy-start(f32[2048]{0:T(1024)} %param.21) | copy-start | bytes 24580
  146.4 32.8 %all-to-all-start.3 = ((bf16[16,32,2048]{2,1,0:T(8,128)(2,1)}), bf16[16,32,2048]{2,1,0:T(8,128)(2,1)}, u32[]{:S(2)}, u32[]{:S(2)}) async-start(bf16[16,32,2048]{2,1,0:T(8,128)(2,1)} %bitcast.108), calls=%async_computation.3 | async-start | bytes 4194304 | tf_op jit(solution)/shard_map/all_to_all | solution.py:133
  156.2 2.2 copy-start.4
  190.6 3.3 copy-start.10
  192.2 3.2 copy-start.6
  210.5 110.7 %all-to-all-start.4 = ((bf16[16,32,2048]{2,1,0:T(8,128)(2,1)}), bf16[16,32,2048]{2,1,0:T(8,128)(2,1)}, u32[]{:S(2)}, u32[]{:S(2)}) async-start(bf16[16,32,2048]{2,1,0:T(8,128)(2,1)} %bitcast.107), calls=%async_computation.4 | async-start | bytes 4194304 | tf_op jit(solution)/shard_map/all_to_all | solution.py:182
  217.5 73.9 %all-reduce.5.cloned.1.call-start = ((), (), s32[]{:S(2)}) async-start(), calls=%async_computation.7 | async-start | bytes 262144 | tf_op jit(solution)/shard_map/psum | solution.py:36
  219.7 101.5 %all-reduce.7.cloned.1.call-start = ((), (), s32[]{:S(2)}) async-start(), calls=%async_computation.8 | async-start | bytes 262144 | tf_op jit(solution)/shard_map/psum | solution.py:36
  291.4 78.5 %all-reduce.9.cloned.1.call-start = ((), (), s32[]{:S(2)}) async-start(), calls=%async_computation.9 | async-start | bytes 262144 | tf_op jit(solution)/shard_map/psum | solution.py:36
  321.2 125.3 %reduce-scatter.4.cloned.1.call-start = ((), (), s32[]{:S(2)}) async-start(), calls=%async_computation.12 | async-start | bytes 10027008
  321.3 3.8 copy-start.19
  325.1 3.6 copy-start.8
  325.1 3.6 copy-start.21
  328.7 1.9 copy-start.23
  349.3 145.4 %all-reduce.11.cloned.1.call-start = ((), (), s32[]{:S(2)}) async-start(), calls=%async_computation.10 | async-start | bytes 262144 | tf_op jit(solution)/shard_map/psum | solution.py:36
  447.9 48.4 %copy-start.1 = (bf16[2048,16]{0,1:T(8,128)(2,1)S(1)}, bf16[2048,16]{0,1:T(8,128)(2,1)}, u32[]{:S(2)}) copy-start(bf16[2048,16]{0,1:T(8,128)(2,1)} %param.17) | copy-start | bytes 196612
  (3 other events, 3.3 us)
Sparse Core Ops, SparseCore 0:
  10.4 57.7 all-gather.5
  70.0 71.3 all-gather.7
  221.2 70.1 all-reduce.4
  294.0 27.1 all-reduce.6
  323.5 46.4 all-reduce.8
  372.4 74.1 reduce-scatter.3
  448.8 45.7 all-reduce.10
